TPU v7x, 128 devices: a whole 4x4x4 slice. The times are simulated.
128 devices in a mesh: patch: 32 (over x, y, z_lo), head: 4 (over z_hi, core).
Axes of the slice: x: 4, y: 4, z: 4 (z_hi: 2, z_lo: 2; z = z_hi * 2 + z_lo), core: 2. Of those that a mesh axis runs over, the one named last changes fastest.
Arguments:
- feature: bfloat16 [128, 96, 1280], P('patch', None, 'head'), may hold values from -6 to 6
- prev_feature: bfloat16 [128, 96, 1280], P('patch', None, 'head'), may hold values from -60 to 60, as said below
- conv_weight: bfloat16 [3, 3, 1280, 1280], P(None, None, None, 'head'), may hold values from -0.0546875 to 0.0546875
- w_query: bfloat16 [1280, 1280], P(None, 'head'), may hold values from -0.15625 to 0.15625
- w_key: bfloat16 [1280, 1280], P(None, 'head'), may hold values from -0.5 to 0.5
- w_value: bfloat16 [1280, 1280], P(None, 'head'), may hold values from -0.3125 to 0.3125
- w_out: bfloat16 [1280, 1280], P('head'), may hold values from -0.15625 to 0.15625
- prev_keys: bfloat16 [12288, 1280], P('patch', 'head'), may hold values from -300 to 300
- prev_values: bfloat16 [12288, 1280], P('patch', 'head'), may hold values from -8 to 8
Outputs:
- resnet_out: float32 [128, 96, 1280], P('patch', None, 'head')
- attended: float32 [12288, 1280], P('patch', 'head')
Inputs may be any that keep to these rules, and one draw needn't show every extreme that they name: `prev_feature`: the previous step's feature map.
All inputs are finite; a program needn't handle non-finite values.
Results may differ from a plain program's by a relative error of at most 0.035.
Values may be sent and summed in bfloat16 or wider, within the bound.
A program may use at most 128 MiB of HBM per device.

v0:
```python
import math

import jax
import jax.numpy as jnp
from jax import lax
from jax.sharding import PartitionSpec as P

C = 1280
GROUPS = 32
HEAD_DIM = 64


def padded_2(block, sides, width):
    for axis, dim in sides:
        count = lax.axis_size(axis)
        forward = [(i, i + 1) for i in range(count - 1)]
        backward = [(target, source) for source, target in forward]
        low = lax.ppermute(
            lax.slice_in_dim(block, block.shape[dim] - width, None, axis=dim), axis, forward
        )
        high = lax.ppermute(lax.slice_in_dim(block, 0, width, axis=dim), axis, backward)
        block = jnp.concatenate([low, block, high], axis=dim)
    return block


def activate(values, centre, rstd, local_groups):
    grouped = values.astype(jnp.float32).reshape(values.shape[0], values.shape[1], local_groups, -1)
    scaled = (grouped - centre[:, None]) * rstd[:, None]
    return jax.nn.silu(scaled).reshape(values.shape).astype(jnp.bfloat16)


def layer_scale(flat, sums, squares, width_all):
    mean_tok = sums / width_all
    var_tok = squares / width_all - mean_tok * mean_tok
    return ((flat - mean_tok[:, None]) * lax.rsqrt(var_tok + 1e-05)[:, None]).astype(jnp.bfloat16)


def attend(carry, keys, values, row_first, own_first, queries, scale):
    top, total, summed = carry
    length = keys.shape[0]
    heads_local = queries.shape[1]
    keys3 = keys.reshape(length, heads_local, -1)
    values3 = values.reshape(length, heads_local, -1)
    scores = jnp.einsum("qhd,khd->hqk", queries, keys3, preferred_element_type=jnp.float32) * scale
    row_ids = row_first + jnp.arange(length, dtype=jnp.int32)
    outside = (row_ids < own_first) | (row_ids >= own_first + queries.shape[0])
    scores = jnp.where(outside[None, None, :], scores, -1e30)
    new_top = jnp.maximum(top, jnp.max(scores, axis=-1))
    factor = jnp.exp(top - new_top)
    expo = jnp.exp(scores - new_top[..., None])
    total = total * factor + jnp.sum(expo, axis=-1)
    summed = summed * factor[..., None] + jnp.einsum(
        "hqk,khd->hqd", expo.astype(jnp.bfloat16), values3, preferred_element_type=jnp.float32
    )
    return (new_top, total, summed)


def on_device(
    feature, prev_feature, conv_weight, w_query, w_key, w_value, w_out, prev_keys, prev_values
):
    rows, cols, width = feature.shape
    group_width = C // GROUPS
    local_groups = width // group_width
    stale_in = prev_feature.astype(jnp.float32).reshape(rows * cols, local_groups, group_width)
    part_sum = jnp.sum(stale_in, axis=(0, 2))
    part_sq = jnp.sum(stale_in * stale_in, axis=(0, 2))
    group_sum, group_sq = lax.psum((part_sum, part_sq), "patch")
    count = rows * cols * group_width * lax.axis_size("patch")
    centre = group_sum / count
    rstd = lax.rsqrt(group_sq / count - centre * centre + 1e-05)
    fresh = activate(feature, centre, rstd, local_groups)
    edges = jnp.concatenate([prev_feature[:1], prev_feature[-1:]], 0)
    stale_edges = activate(edges, centre, rstd, local_groups)
    rims = padded_2(stale_edges, (("patch", 0),), 1)
    padded = jnp.concatenate([rims[:1], fresh, rims[-1:]], 0)
    total = jnp.zeros((rows, cols, width), jnp.float32)
    wide = jnp.pad(lax.all_gather(padded, "head", axis=2, tiled=True), ((0, 0), (1, 1), (0, 0)))
    for offset_y in range(3):
        for offset_x in range(3):
            window = wide[offset_y : offset_y + rows, offset_x : offset_x + cols]
            total = total + jnp.einsum(
                "rwc,cd->rwd",
                window,
                conv_weight[offset_y, offset_x],
                preferred_element_type=jnp.float32,
            )
    conv = total
    resnet_out = feature.astype(jnp.float32) + conv
    tok = rows * cols
    flat_out = resnet_out.reshape(tok, width)
    whole = lax.all_gather(flat_out, "head", axis=1, tiled=True)
    normed = layer_scale(
        whole, jnp.sum(whole, axis=1), jnp.sum(whole * whole, axis=1), whole.shape[1]
    )
    query = jnp.dot(normed, w_query, preferred_element_type=jnp.float32).astype(jnp.bfloat16)
    key = jnp.dot(normed, w_key, preferred_element_type=jnp.float32).astype(jnp.bfloat16)
    value = jnp.dot(normed, w_value, preferred_element_type=jnp.float32).astype(jnp.bfloat16)
    heads_local = width // HEAD_DIM
    scale = 1.0 / HEAD_DIM**0.5
    queries = query.reshape(tok, heads_local, HEAD_DIM)
    own_first = lax.axis_index("patch") * tok
    own_scores = (
        jnp.einsum(
            "qhd,khd->hqk",
            queries,
            key.reshape(tok, heads_local, HEAD_DIM),
            preferred_element_type=jnp.float32,
        )
        * scale
    )
    top = jnp.max(own_scores, axis=-1)
    expo = jnp.exp(own_scores - top[..., None])
    carry = (
        top,
        jnp.sum(expo, axis=-1),
        jnp.einsum(
            "hqk,khd->hqd",
            expo.astype(jnp.bfloat16),
            value.reshape(tok, heads_local, HEAD_DIM),
            preferred_element_type=jnp.float32,
        ),
    )
    keys_all, values_all = (
        lax.all_gather(prev_keys, "patch", axis=0, tiled=True),
        lax.all_gather(prev_values, "patch", axis=0, tiled=True),
    )
    state = carry
    pieces = (keys_all, values_all)
    length = pieces[0].shape[0]
    block = math.gcd(length, 2048)
    blocks = length // block
    key_blocks = pieces[0].reshape(blocks, block, width)
    value_blocks = pieces[1].reshape(blocks, block, width)

    def step(inner, item):
        keys, values, index = item
        return (attend(inner, keys, values, index * block, own_first, queries, scale), None)

    state, unused = lax.scan(
        step, state, (key_blocks, value_blocks, jnp.arange(blocks, dtype=jnp.int32))
    )
    carry = state
    top, total, summed = carry
    heads_out = (
        (summed / total[..., None]).transpose(1, 0, 2).reshape(tok, width).astype(jnp.bfloat16)
    )
    partial_out = jnp.dot(heads_out, w_out, preferred_element_type=jnp.float32)
    attended = lax.psum_scatter(partial_out, "head", scatter_dimension=1, tiled=True)
    return (resnet_out, attended)


def solution(mesh):
    placed = (
        P("patch", None, "head"),
        P("patch", None, "head"),
        P(None, None, None, "head"),
        P(None, "head"),
        P(None, "head"),
        P(None, "head"),
        P("head", None),
        P("patch", "head"),
        P("patch", "head"),
    )
    return jax.shard_map(
        on_device,
        mesh=mesh,
        in_specs=placed,
        out_specs=(P("patch", None, "head"), P("patch", "head")),
        check_vma=False,
    )
```

profile of v0, /device:TPU:1, one launch (start us, length us, event | category | flops | bytes accessed | tf_op | source)
XLA Modules:
  0.0 700.3 jit_solution(843146869598454087)
XLA Ops:
  9.7 70.0 %all-reduce.1 = (f32[8]{0:T(128)S(1)}, f32[8]{0:T(128)S(1)}) all-reduce(f32[8]{0:T(128)S(1)} %reduce_sum.74, f32[8]{0:T(128)S(1)} %reduce_sum.71), channel_id=1, replica_groups=mesh['patch'=32,'head'=4] {'patch'}, use_global_device_ids=true, to_apply=%region_5.6 | all-reduce | flops 16 | bytes 128 | tf_op jit(solution)/shard_map/psum | solution.py:67
  88.0 42.8 %all-gather.5.cloned.1.call-done = bf16[6,96,1280]{1,0,2:T(8,128)(2,1)} async-done(((bf16[6,96,320]{1,0,2:T(8,128)(2,1)}), bf16[6,96,1280]{1,0,2:T(8,128)(2,1)}) %all-gather.5.cloned.1.call-update) | async-done | bytes 1474576 | tf_op jit(solution)/shard_map/all_gather | solution.py:77
  153.4 24.0 %all-gather.7.cloned.1.call-done = f32[384,1280]{0,1:T(8,128)} async-done(((f32[384,320]{0,1:T(8,128)}), f32[384,1280]{0,1:T(8,128)}) %all-gather.7.cloned.1.call-update) | async-done | bytes 1966096 | tf_op jit(solution)/shard_map/all_gather | solution.py:91
  184.5 169.7 %all-gather.11.cloned.1.call-done = bf16[12288,320]{0,1:T(8,128)(2,1)} async-done(((bf16[384,320]{0,1:T(8,128)(2,1)}), bf16[12288,320]{0,1:T(8,128)(2,1)}) %all-gather.11.cloned.1.call-update) | async-done | bytes 7864336 | tf_op jit(solution)/shard_map/all_gather | solution.py:125
  354.2 11.6 %copy.40 = bf16[12288,320]{1,0:T(8,128)(2,1)} copy(bf16[12288,320]{0,1:T(8,128)(2,1)} %all-gather.11.cloned.1.call-done) | data formatting | bytes 15728640 | tf_op jit(solution)/shard_map/all_gather | solution.py:125
  365.9 11.7 %copy.42 = bf16[6,2048,320]{1,2,0:T(8,128)(2,1)} copy(bf16[6,2048,320]{2,1,0:T(8,128)(2,1)} %bitcast.105) | data formatting | bytes 15728640 | tf_op jit(solution)/shard_map/while | solution.py:139
  377.5 157.3 %all-gather.9.cloned.1.call-done = bf16[12288,320]{0,1:T(8,128)(2,1)} async-done(((bf16[384,320]{0,1:T(8,128)(2,1)}), bf16[12288,320]{0,1:T(8,128)(2,1)}) %all-gather.9.cloned.1.call-update) | async-done | bytes 7864336 | tf_op jit(solution)/shard_map/all_gather | solution.py:124
  534.8 11.6 %copy.39 = bf16[12288,320]{1,0:T(8,128)(2,1)} copy(bf16[12288,320]{0,1:T(8,128)(2,1)} %all-gather.9.cloned.1.call-done) | data formatting | bytes 15728640 | tf_op jit(solution)/shard_map/all_gather | solution.py:124
  546.4 11.6 %copy.41 = bf16[6,2048,320]{1,2,0:T(8,128)(2,1)} copy(bf16[6,2048,320]{2,1,0:T(8,128)(2,1)} %bitcast.106) | data formatting | bytes 15728640 | tf_op jit(solution)/shard_map/while | solution.py:139
  558.0 92.8 %while.15 = (s32[]{:T(128)}, f32[5,384]{1,0:T(8,128)S(1)}, f32[5,384]{1,0:T(8,128)S(1)}, f32[5,384,64]{1,2,0:T(8,128)S(1)}, s32[6]{0:T(128)S(1)}, /*index=5*/s32...) while((s32[]{:T(128)}, f32[5,384]{1,0:T(8,128)S(1)}, ...), condition=%wide.region_13.14_spmd, body=%wide.region_10.13_spmd.sunk | while | flops 1050144512 | bytes 56410276 | solution.py:139
  561.2 4.2 bitcast_reduce_fusion.2
  565.5 4.2 fusion.110
  569.7 3.7 fusion.111
  576.7 4.2 bitcast_reduce_fusion.2
  580.9 4.2 fusion.110
  592.2 4.2 bitcast_reduce_fusion.2
  596.4 4.2 fusion.110
  607.6 4.2 bitcast_reduce_fusion.2
  611.9 4.2 fusion.110
  623.1 4.2 bitcast_reduce_fusion.2
  627.3 4.2 fusion.110
  638.6 4.2 bitcast_reduce_fusion.2
  642.8 4.2 fusion.110
  653.0 40.8 %reduce-scatter.2.cloned.1.call-done = f32[384,320]{0,1:T(8,128)} async-done(((f32[384,1280]{0,1:T(8,128)}), f32[384,320]{0,1:T(8,128)}) %reduce-scatter.2.cloned.1.call-update) | async-done | bytes 491536 | tf_op jit(solution)/shard_map/reduce_scatter | solution.py:148
  (106 shorter events, 76.4 us)
Async XLA Ops:
  7.2 643.7 %copy-start = (bf16[320,1280]{1,0:T(8,128)(2,1)S(1)}, bf16[320,1280]{1,0:T(8,128)(2,1)}, u32[]{:S(2)}) copy-start(bf16[320,1280]{1,0:T(8,128)(2,1)} %param.17) | copy-start | bytes 2457604
  7.2 123.6 %all-gather.5.cloned.1.call-start = ((), (), s32[]{:S(2)}) async-start(), calls=%async_computation.1 | async-start | bytes 3276800 | tf_op jit(solution)/shard_map/all_gather | solution.py:77
  80.2 3.8 collective-permute-start
  81.5 5.1 collective-permute-start.1
  88.0 89.4 %all-gather.7.cloned.1.call-start = ((), (), s32[]{:S(2)}) async-start(), calls=%async_computation.2 | async-start | bytes 2457600 | tf_op jit(solution)/shard_map/all_gather | solution.py:91
  147.2 1.9 copy-start.3
  151.0 28.8 %copy-start.2 = (f32[4,96,320]{2,1,0:T(8,128)}, f32[4,96,320]{2,1,0:T(8,128)S(1)}, u32[]{:S(2)}) copy-start(f32[4,96,320]{2,1,0:T(8,128)S(1)} %fusion.21) | copy-start | bytes 1474564
  152.0 202.2 %all-gather.11.cloned.1.call-start = ((), (), s32[]{:S(2)}) async-start(), calls=%async_computation.4 | async-start | bytes 8110080 | tf_op jit(solution)/shard_map/all_gather | solution.py:125
  152.8 382.0 %all-gather.9.cloned.1.call-start = ((), (), s32[]{:S(2)}) async-start(), calls=%async_computation.3 | async-start | bytes 8110080 | tf_op jit(solution)/shard_map/all_gather | solution.py:124
  153.3 540.4 %reduce-scatter.2.cloned.1.call-start = ((), (), s32[]{:S(2)}) async-start(), calls=%async_computation.5 | async-start | bytes 2457600 | tf_op jit(solution)/shard_map/reduce_scatter | solution.py:148
  177.4 2.1 copy-start.1
  179.4 2.1 copy-start.4
  182.1 1.1 copy-start.5
Sparse Core Ops, SparseCore 0:
  88.1 42.6 all-gather.4
  152.1 25.2 all-gather.6
  179.1 175.1 all-gather.10
  355.7 179.0 all-gather.8
  653.1 40.6 reduce-scatter.1
where the time goes:
time: 702 us; the launch traced here: 700 us
  waiting for transfers between devices  438 us (62%)
  matrix products  70.4 us (10%)
  blocking collectives  70 us (10%)
  local copies, waits for them, and re-layouts  69.2 us (10%)
  other arithmetic  31 us (4%)
  between operations  14 us (2%)
    all_gather x1, waiting for transfers between devices, on_device(): lax.all_gather(prev_values, 'patch', axis=0, tiled=True)  170 us
    all_gather x1, waiting for transfers between devices, on_device(): lax.all_gather(prev_keys, 'patch', axis=0, tiled=True)  157 us
    psum x1, blocking collectives, on_device(): group_sum, group_sq = lax.psum((part_sum, part_sq), 'patch')  70 us
    all_gather x1, waiting for transfers between devices, on_device(): lax.all_gather(padded, 'head', axis=2, tiled=True)  42.8 us
    reduce_scatter x1, waiting for transfers between devices, on_device(): lax.psum_scatter(partial_out, 'head', scatter_dimension=1, tiled=True)  40.8 us
    reduce_sum x6, other arithmetic, attend(): total = total * factor + jnp.sum(expo, axis=-1)  25.4 us
    dot_general x6, matrix products, attend(): jnp.einsum('qhd,khd->hqk', queries, keys3, preferred_element_type=jnp.flo...  25.4 us
    all_gather x1, waiting for transfers between devices, on_device(): whole = lax.all_gather(flat_out, 'head', axis=1, tiled=True)  24 us
  transfers between devices with their start and end apart: 7, of which 6 were waited for; matrix products, arithmetic and copies ran while one was open for 4% of the time, Pallas kernels for 0%

commit v1 on v0

v1 whole, which is shorter than its diff:
```python
import functools

import jax
import jax.numpy as jnp
from jax import lax
from jax.experimental import pallas as pl
from jax.experimental.pallas import tpu as pltpu
from jax.sharding import PartitionSpec as P

C = 1280
GROUPS = 32
HEAD_DIM = 64
TOK = 384
COLS = 96
WIDTH = 320
HEADS_DEV = 5
CHUNK = 4 * TOK
FIRST_OWN = 0
FIRST_OTHER = TOK
SECOND = 5 * TOK
PLACE = {0: 4, 1: 1, 2: 2, 3: 3, 4: 5, 5: 6, 6: 7, 7: 8}
NT = (((1,), (1,)), ((), ()))
N_PATCH = 32
COUNT = 128 * 96 * (C // GROUPS)
SCORE_SCALE = 1.4426950408889634 / HEAD_DIM**0.5
BF16 = jnp.bfloat16
F32 = jnp.float32
MESH = pl.DeviceIdType.MESH

SEM_FEATURE = 0
SEM_ROWS = 6
SEM_RIMS = 10
SEM_TOKENS = 12
SEM_W_OUT = 24
SEM_STATS_HEAD = 27
SEM_STATS_KEY = 30
SEM_STATS_QUERY = 37
SEM_QUERY = 40
SEM_KEY = 43
SEM_VALUE = 51
SEM_PARTIAL = 59
SEM_LEVEL = 74
SEM_HEADS = 89
SEMS = 109


def kernel(
    feature,
    prev_feature,
    conv_weight,
    w_query,
    w_key,
    w_value,
    w_out,
    prev_keys,
    prev_values,
    resnet_ref,
    attended_ref,
    raw,
    prev_in,
    sums_own,
    sums_key,
    sums_query,
    sums_head,
    groups,
    slopes,
    act,
    conv_w,
    qkv_w,
    conv_part,
    res_out,
    tokens,
    normed,
    queries,
    query_heads,
    key_t,
    value_t,
    scores,
    tops,
    part,
    partial_out,
    partial_in,
    level_out,
    level_in,
    relay_feature,
    relay_tokens,
    relay_heads,
    heads,
    out_w,
    out_w_send,
    out_w_rows,
    attended,
    send,
    recv,
    local,
):
    p = lax.axis_index("patch")
    h = lax.axis_index("head")
    x, y, zl = p // 8, (p // 2) % 4, p % 2

    def at(xx, yy, zz):
        return xx * 8 + yy * 2 + zz

    xn = x + 1 - 2 * (x % 2)
    xf = (x + 2) % 4
    y1, y2, y3 = (y + 1) % 4, (y + 2) % 4, (y + 3) % 4
    zh, core = h // 2, h % 2
    h_chip = zh * 2 + 1 - core
    h_far = (1 - zh) * 2 + core
    h_diag = (1 - zh) * 2 + 1 - core
    h_up = ((zh + zl) % 2) * 2 + core
    h_down = ((zh + 1 - zl) % 2) * 2 + core

    dev_chip, dev_far, dev_diag = (p, h_chip), (p, h_far), (p, h_diag)
    dev_up, dev_down = (at(x, y, 1 - zl), h_up), (at(x, y, 1 - zl), h_down)
    key_peers = [
        (at(x, y1, zl), h),
        (at(x, y3, zl), h),
        (at(x, y2, zl), h),
        (at(xf, y, zl), h),
        (at(xf, y1, zl), h),
        (at(xf, y3, zl), h),
        (at(xf, y2, zl), h),
    ]
    dev_y1, dev_y3, dev_y2, dev_xf = key_peers[:4]
    query_peers = [(at(x, y, 1 - zl), h), (at(xn, y, zl), h), (at(xn, y, 1 - zl), h)]
    p_next, p_prev = (p + 1) % N_PATCH, (p + N_PATCH - 1) % N_PATCH
    rim_peers = [(p_next, h), (p_next, h_far), (p_prev, h), (p_prev, h_far)]

    started = []

    def copy(src, dst, sem_send, sem_recv, device):
        return pltpu.make_async_remote_copy(
            src_ref=src,
            dst_ref=dst,
            send_sem=send.at[sem_send],
            recv_sem=recv.at[sem_recv],
            device_id=device,
            device_id_type=MESH,
        )

    def push(src, dst, sem, device, sem_send=None):
        c = copy(src, dst, sem if sem_send is None else sem_send, sem, device)
        c.start()
        started.append(c)

    def arrived(dst, sem, device):
        copy(dst, dst, sem, sem, device).wait_recv()

    def fetch(src, dst, sem):
        c = pltpu.make_async_copy(src, dst, local.at[sem])
        c.start()
        return c

    def columns(slot):
        return slice(PLACE[slot] * TOK, (PLACE[slot] + 1) * TOK)

    def key_slot(slot):
        return key_t.at[:, 0:HEAD_DIM, columns(slot)]

    def value_slot(slot):
        return value_t.at[:, 0:HEAD_DIM, columns(slot)]

    load_feature = fetch(feature, raw.at[h, 0:TOK], 0)
    load_prev = fetch(prev_feature, prev_in, 1)
    load_keys = fetch(prev_keys, key_slot(0), 2)
    load_values = fetch(prev_values, value_slot(0), 3)
    load_conv = fetch(conv_weight, conv_w, 4)
    load_q = fetch(w_query, qkv_w.at[0], 5)
    load_k = fetch(w_key, qkv_w.at[1], 6)
    load_v = fetch(w_value, qkv_w.at[2], 7)
    load_o = fetch(w_out, out_w, 8)

    barrier = pltpu.get_barrier_semaphore()
    peers = [dev_chip, dev_far, dev_diag, dev_up, dev_down]
    peers += key_peers + query_peers + rim_peers
    for peer in peers:
        pl.semaphore_signal(barrier, inc=1, device_id=peer, device_id_type=MESH)

    load_prev.wait()
    stale = prev_in[...].astype(F32)
    sums_own[0] = jnp.zeros((8, WIDTH), F32)
    sums_own[0, 0:1] = jnp.sum(stale, axis=0, keepdims=True)
    sums_own[0, 1:2] = jnp.sum(stale * stale, axis=0, keepdims=True)
    key_t[:, HEAD_DIM : 2 * HEAD_DIM, :] = jnp.zeros((HEADS_DEV, HEAD_DIM, 9 * TOK), BF16)
    query_heads[...] = jnp.zeros(query_heads.shape, BF16)
    value_t[:, HEAD_DIM : 2 * HEAD_DIM, :] = jnp.ones((HEADS_DEV, HEAD_DIM, 9 * TOK), BF16)
    load_o.wait()
    for i in range(4):
        out_w_send[i] = out_w[:, i * WIDTH : (i + 1) * WIDTH].T
    out_w_rows[h] = out_w_send[h]
    load_feature.wait()
    load_keys.wait()
    load_values.wait()

    row_group = (lax.broadcasted_iota(jnp.int32, (WIDTH, WIDTH), 0) * 1639) >> 16
    col_group = (lax.broadcasted_iota(jnp.int32, (WIDTH, WIDTH), 1) * 1639) >> 16
    same_group = jnp.where(row_group == col_group, 1.0, 0.0).astype(F32)
    groups[...] = same_group
    pl.semaphore_wait(barrier, len(peers))

    def relay_start(up, down, relay_up, relay_down, sem):
        push(up, relay_up, sem, dev_up)
        push(down, relay_down, sem + 1, dev_down)

    def relay_on(relay_up, relay_down, far_up, far_down, sem):
        arrived(relay_up, sem, dev_down)
        push(relay_up, far_up, sem + 2, dev_up)
        arrived(relay_down, sem + 1, dev_up)
        push(relay_down, far_down, sem + 3, dev_down)

    def relay_end(up, down, whole, sem):
        arrived(up, sem + 2, dev_down)
        arrived(down, sem + 3, dev_up)
        push(whole, whole, sem + 5, dev_chip)

    half = TOK // 2

    for i, peer in enumerate(key_peers):
        push(sums_own.at[0], sums_key.at[i], SEM_STATS_KEY + i, peer)

    relay_start(
        raw.at[h, 0:half],
        raw.at[h, half:TOK],
        relay_feature.at[0],
        relay_feature.at[1],
        SEM_FEATURE,
    )
    push(raw.at[h, 0:TOK], raw.at[h, 0:TOK], SEM_FEATURE + 4, dev_chip)
    above, below = slice(TOK, TOK + COLS), slice(TOK + COLS, TOK + 2 * COLS)
    for i in range(2):
        push(prev_in.at[TOK - COLS : TOK], raw.at[h, above], SEM_ROWS + i, rim_peers[i])
        push(prev_in.at[0:COLS], raw.at[h, below], SEM_ROWS + 2 + i, rim_peers[2 + i])

    total = sums_own[0]
    for i, peer in enumerate(key_peers):
        arrived(sums_key.at[i], SEM_STATS_KEY + i, peer)
        total = total + sums_key[i]
    sums_own[1] = total
    for i, peer in enumerate(query_peers):
        push(sums_own.at[1], sums_query.at[i], SEM_STATS_QUERY + i, peer)

    for i, peer in enumerate(query_peers):
        arrived(sums_query.at[i], SEM_STATS_QUERY + i, peer)
        total = total + sums_query[i]
    sums_head[h] = total
    head_peers = ((dev_chip, h_chip), (dev_far, h_far), (dev_diag, h_diag))
    for i, (peer, other) in enumerate(head_peers):
        push(sums_head.at[h], sums_head.at[h], SEM_STATS_HEAD + i, peer)

    def push_key(src, slot, device):
        push(src, key_slot(slot), SEM_KEY + slot, device)

    def push_value(src, slot, device):
        push(src, value_slot(slot), SEM_VALUE + slot, device)

    for slot, peer in ((3, dev_xf), (2, dev_y1), (1, dev_y3)):
        push_key(key_slot(0), slot, peer)
        push_value(value_slot(0), slot, peer)

    relay_on(
        relay_feature.at[0],
        relay_feature.at[1],
        raw.at[h_down, 0:half],
        raw.at[h_up, half:TOK],
        SEM_FEATURE,
    )
    for i, other in enumerate((h, h_far)):
        arrived(raw.at[other, above], SEM_ROWS + i, rim_peers[2 + i])
        arrived(raw.at[other, below], SEM_ROWS + 2 + i, rim_peers[i])
        rims = raw.at[other, TOK : TOK + 2 * COLS]
        push(rims, rims, SEM_RIMS + i, dev_chip)

    for i, (peer, other) in enumerate(head_peers):
        arrived(sums_head.at[other], SEM_STATS_HEAD + i, peer)
    group_sums = (
        jnp.dot(
            sums_head[...].reshape(32, WIDTH),
            groups[...],
            precision=lax.Precision.HIGHEST,
            preferred_element_type=F32,
        )
        * (1.0 / COUNT)
    )

    for i in range(4):
        centre = group_sums[8 * i : 8 * i + 1]
        square = group_sums[8 * i + 1 : 8 * i + 2]
        rstd = 0.5 * lax.rsqrt(square - centre * centre + 1e-05)
        slopes[i, 0:1] = rstd
        slopes[i, 1:2] = -centre * rstd

    def rims_of(other):
        return raw.at[other, TOK : TOK + 2 * COLS]

    arrived(rims_of(h_chip), SEM_RIMS, dev_chip)
    arrived(raw.at[h_chip, 0:TOK], SEM_FEATURE + 4, dev_chip)

    def activate(chip, place, src, dst, rows, inside):
        for c in range(2):
            i = chip * 2 + c
            v = raw[i, pl.ds(src, rows)].astype(F32) * slopes[i, 0:1] + slopes[i, 1:2]
            v = v + v * jnp.tanh(v)
            if inside is not None:
                v = jnp.where(inside, v, 0.0)
            act[place, pl.ds(dst, rows), c * WIDTH : (c + 1) * WIDTH] = v.astype(BF16)

    def activate_chip(chip, place):
        def body(t, carry):
            first = pl.multiple_of(t * 48, 48)
            activate(chip, place, first, pl.multiple_of(first + COLS, 48), 48, None)
            return carry

        lax.fori_loop(0, 8, body, 0)
        activate(chip, place, TOK, 0, COLS, p > 0)
        activate(chip, place, TOK + COLS, TOK + COLS, COLS, p < N_PATCH - 1)

    def convolve(place, chip, first, count):
        channels = pl.ds(pl.multiple_of(chip * (C // 2), 128), C // 2)

        def body(dx, carry):
            total = None
            for dy in range(3):
                product = lax.dot_general(
                    act[place, first + dy * COLS : first + dy * COLS + count],
                    conv_w[dy * 3 + dx, :, channels],
                    NT,
                    preferred_element_type=F32,
                )
                total = product if total is None else total + product
            if place == 0:
                conv_part[dx, first : first + count] = total
            else:
                conv_part[dx, first : first + count] += total
            return carry

        lax.fori_loop(0, 3, body, 0)

    activate_chip(zh, 0)
    load_conv.wait()
    relay_end(raw.at[h_far, 0:half], raw.at[h_far, half:TOK], raw.at[h_far, 0:TOK], SEM_FEATURE)
    convolve(0, zh, 0, TOK)
    arrived(rims_of(h_diag), SEM_RIMS + 1, dev_chip)
    arrived(raw.at[h_diag, 0:TOK], SEM_FEATURE + 5, dev_chip)
    activate_chip(1 - zh, 1)

    def conv_half(part_of):
        first = part_of * half
        convolve(1, 1 - zh, first, half)

        def merge_body(t, carry):
            rows = pl.ds(pl.multiple_of(t * COLS, COLS), COLS)
            col = lax.broadcasted_iota(jnp.int32, (COLS, WIDTH), 0)
            left = jnp.where(col == 0, 0.0, pltpu.roll(conv_part[0, rows], 1, axis=0))
            right = jnp.where(
                col == COLS - 1, 0.0, pltpu.roll(conv_part[2, rows], COLS - 1, axis=0)
            )
            result = raw[h, rows].astype(F32) + (conv_part[1, rows] + left + right)
            res_out[rows] = result
            tokens[h, rows] = result.astype(BF16)
            return carry

        lax.fori_loop(2 * part_of, 2 * part_of + 2, merge_body, 0)
        middle, last = first + COLS, first + half
        sem = SEM_TOKENS + 6 * part_of
        relay_start(
            tokens.at[h, first:middle],
            tokens.at[h, middle:last],
            relay_tokens.at[0, part_of],
            relay_tokens.at[1, part_of],
            sem,
        )
        push(tokens.at[h, first:last], tokens.at[h, first:last], sem + 4, dev_chip)

    def tokens_on(part_of):
        first, middle = part_of * half, part_of * half + COLS
        relay_on(
            relay_tokens.at[0, part_of],
            relay_tokens.at[1, part_of],
            tokens.at[h_down, first:middle],
            tokens.at[h_up, middle : first + half],
            SEM_TOKENS + 6 * part_of,
        )

    def tokens_end(part_of):
        first, middle, last = part_of * half, part_of * half + COLS, part_of * half + half
        relay_end(
            tokens.at[h_far, first:middle],
            tokens.at[h_far, middle:last],
            tokens.at[h_far, first:last],
            SEM_TOKENS + 6 * part_of,
        )

    def tokens_come(part_of):
        rows, sem = slice(part_of * half, part_of * half + half), SEM_TOKENS + 6 * part_of
        arrived(tokens.at[h_chip, rows], sem + 4, dev_chip)
        arrived(tokens.at[h_diag, rows], sem + 5, dev_chip)

    conv_half(0)
    arrived(key_slot(2), SEM_KEY + 2, dev_y3)
    push_key(key_slot(2), 4, dev_y1)
    arrived(value_slot(1), SEM_VALUE + 1, dev_y1)
    push_value(value_slot(1), 4, dev_y3)
    conv_half(1)
    store_resnet = fetch(res_out, resnet_ref, 9)
    tokens_on(0)
    arrived(key_slot(3), SEM_KEY + 3, dev_xf)
    push_key(key_slot(3), 6, dev_y1)
    push_key(key_slot(3), 5, dev_y3)
    arrived(value_slot(3), SEM_VALUE + 3, dev_xf)
    push_value(value_slot(3), 6, dev_y1)
    push_value(value_slot(3), 5, dev_y3)
    tokens_on(1)
    tokens_end(0)
    tokens_end(1)
    tokens_come(0)
    tokens_come(1)

    def norm_body(t, carry):
        rows = pl.ds(pl.multiple_of(t * COLS, COLS), COLS)
        parts = [tokens[i, rows].astype(F32) for i in range(4)]
        mean = sum(jnp.sum(v, axis=1, keepdims=True) for v in parts) * (1.0 / C)
        square = sum(jnp.sum(v * v, axis=1, keepdims=True) for v in parts) * (1.0 / C)
        rstd = lax.rsqrt(square - mean * mean + 1e-05)
        for i in range(4):
            normed[rows, i * WIDTH : (i + 1) * WIDTH] = ((parts[i] - mean) * rstd).astype(BF16)
        return carry

    lax.fori_loop(0, 4, norm_body, 0)

    def split_heads(slot):
        for i in range(HEADS_DEV):
            query_heads[slot, i, :, 0:HEAD_DIM] = queries[slot, i].T

    def project_tokens(i):
        result = lax.dot_general(qkv_w[i], normed[...], NT, preferred_element_type=F32)
        return result.astype(BF16).reshape(HEADS_DEV, HEAD_DIM, TOK)

    load_q.wait()
    queries[0] = project_tokens(0)
    for i, peer in enumerate(query_peers[:2]):
        push(queries.at[0], queries.at[i + 1], SEM_QUERY + i, peer)
    load_k.wait()
    key_t[:, 0:HEAD_DIM, 0:TOK] = project_tokens(1)
    load_v.wait()
    value_t[:, 0:HEAD_DIM, 0:TOK] = project_tokens(2)
    split_heads(0)

    lane = lax.broadcasted_iota(jnp.int32, (128, 128), 1)

    def score_rows(slot, first, i, t):
        rows = slice(t * 128, (t + 1) * 128)
        result = jnp.dot(
            query_heads[slot, i, rows],
            key_t[i, :, first : first + CHUNK],
            preferred_element_type=F32,
        )
        scores[t] = result
        tops[t] = functools.reduce(
            jnp.maximum, [result[:, 128 * k : 128 * (k + 1)] for k in range(CHUNK // 128)]
        )

    def weigh_rows(slot, first, i, t):
        rows = slice(t * 128, (t + 1) * 128)
        top = jnp.max(tops[t], axis=1, keepdims=True) * SCORE_SCALE
        weights = jnp.exp2(scores[t] * SCORE_SCALE - top).astype(BF16)
        summed = lax.dot_general(
            weights, value_t[i, :, first : first + CHUNK], NT, preferred_element_type=F32
        )
        turned = jnp.where(lane == 65, top, summed).T
        if first != SECOND:
            part[slot, i, :, rows] = turned[0:72]
            return
        before = part[slot, i, :, rows]
        level = jnp.maximum(before[65:66], turned[65:66])
        both = before[0:65] * jnp.exp2(before[65:66] - level) + turned[0:65] * jnp.exp2(
            turned[65:66] - level
        )
        result = both[0:64] / both[64:65]
        lse = level + jnp.log2(both[64:65])
        if slot == 0:
            part[0, i, 0:64, rows] = result
        else:
            partial_out[slot - 1, i, :, rows] = result.astype(BF16)
        level_out[slot, i, :, rows] = jnp.broadcast_to(lse, (8, 128))

    def partial_copies(slot, i):
        n = (slot - 1) * HEADS_DEV + i
        return (
            copy(
                partial_out.at[slot - 1, i],
                partial_in.at[slot - 1, i],
                SEM_PARTIAL + n,
                SEM_PARTIAL + n,
                query_peers[slot - 1],
            ),
            copy(
                level_out.at[slot, i],
                level_in.at[slot - 1, i],
                SEM_LEVEL + n,
                SEM_LEVEL + n,
                query_peers[slot - 1],
            ),
        )

    def send_partial(slot, first, i):
        if slot > 0 and first == SECOND:
            for c in partial_copies(slot, i):
                c.start()

    steps = [(0, FIRST_OWN)]
    steps += [(slot, FIRST_OTHER) for slot in (1, 2, 3)]
    steps += [(slot, SECOND) for slot in (3, 2, 1, 0)]

    def attend(step):
        slot, first = steps[step]

        def body(i, carry):
            score_rows(slot, first, i, 1)
            weigh_rows(slot, first, i, 0)
            score_rows(slot, first, i, 2)
            weigh_rows(slot, first, i, 1)
            score_rows(slot, first, i + 1, 0)
            weigh_rows(slot, first, i, 2)
            send_partial(slot, first, i)
            return carry

        lax.fori_loop(0, HEADS_DEV - 1, body, 0)

    def attend_head(slot, first, i, following):
        def body(unused, carry):
            score_rows(slot, first, i, 1)
            weigh_rows(slot, first, i, 0)
            score_rows(slot, first, i, 2)
            weigh_rows(slot, first, i, 1)
            if following is not None:
                score_rows(*following, 0)
            weigh_rows(slot, first, i, 2)
            send_partial(slot, first, i)
            return carry

        lax.fori_loop(0, 1, body, 0)

    def attend_last(step):
        attend_head(*steps[step], HEADS_DEV - 1, (*steps[step + 1], 0))

    def combine(i):
        for r in range(3):
            for c in partial_copies(r + 1, i):
                c.wait_recv()
        levels = [level_out[0, i, 0:1]] + [level_in[r, i, 0:1] for r in range(3)]
        top = functools.reduce(jnp.maximum, levels)
        shares = [jnp.exp2(level - top) for level in levels]
        whole = 1.0 / sum(shares)
        result = part[0, i, 0:64] * (shares[0] * whole)
        for r in range(3):
            result = result + partial_in[r, i].astype(F32) * (shares[r + 1] * whole)
        heads[h, i] = result.astype(BF16)
        push(heads.at[h, i], relay_heads.at[i], SEM_HEADS + i, dev_down if i % 2 else dev_up)
        push(heads.at[h, i], heads.at[h, i], SEM_HEADS + 10 + i, dev_chip)

    def heads_on(i):
        source, target = (dev_up, dev_down) if i % 2 else (dev_down, dev_up)
        arrived(relay_heads.at[i], SEM_HEADS + i, source)
        far = heads.at[h_up if i % 2 else h_down, i]
        push(relay_heads.at[i], far, SEM_HEADS + 5 + i, target)

    def heads_end(i):
        far = heads.at[h_far, i]
        arrived(far, SEM_HEADS + 5 + i, dev_up if i % 2 else dev_down)
        push(far, far, SEM_HEADS + 15 + i, dev_chip)

    arrived(key_slot(1), SEM_KEY + 1, dev_y1)
    arrived(value_slot(2), SEM_VALUE + 2, dev_y3)
    score_rows(0, FIRST_OWN, 0, 0)
    attend(0)
    arrived(key_slot(6), SEM_KEY + 6, dev_y3)
    push_key(key_slot(6), 7, dev_y1)
    arrived(value_slot(5), SEM_VALUE + 5, dev_y1)
    push_value(value_slot(5), 7, dev_y3)
    push(queries.at[0], queries.at[3], SEM_QUERY + 2, query_peers[2])

    for step in range(1, 4):
        arrived(queries.at[step], SEM_QUERY + step - 1, query_peers[step - 1])
        split_heads(step)
        attend_last(step - 1)
        attend(step)
        if step == 2:
            for i, (peer, other) in enumerate(head_peers):
                push(out_w_send.at[other], out_w_rows.at[h], SEM_W_OUT + i, peer)

    arrived(key_slot(5), SEM_KEY + 5, dev_y1)
    arrived(value_slot(6), SEM_VALUE + 6, dev_y3)
    arrived(key_slot(4), SEM_KEY + 4, dev_y3)
    arrived(value_slot(4), SEM_VALUE + 4, dev_y1)
    arrived(key_slot(7), SEM_KEY + 7, dev_y3)
    arrived(value_slot(7), SEM_VALUE + 7, dev_y1)

    for step in range(4, 7):
        attend_last(step - 1)
        attend(step)
    attend_last(6)
    for i in range(HEADS_DEV):
        attend_head(0, SECOND, i, (0, SECOND, i + 1) if i + 1 < HEADS_DEV else None)
        combine(i)
        if i > 0:
            heads_on(i - 1)
        if i > 1:
            heads_end(i - 2)
    heads_on(HEADS_DEV - 1)
    heads_end(HEADS_DEV - 2)

    for i, (peer, other) in enumerate(head_peers):
        arrived(out_w_rows.at[other], SEM_W_OUT + i, peer)

    def project(i):
        return jnp.dot(
            out_w_rows[i], heads[i].reshape(WIDTH, TOK), preferred_element_type=F32
        )

    attended[...] = project(h)
    for i in range(HEADS_DEV):
        arrived(heads.at[h_chip, i], SEM_HEADS + 10 + i, dev_chip)
    attended[...] += project(h_chip)
    heads_end(HEADS_DEV - 1)
    attended[...] += project(h_far)
    for i in range(HEADS_DEV):
        arrived(heads.at[h_diag, i], SEM_HEADS + 15 + i, dev_chip)
    attended[...] += project(h_diag)
    store_attended = fetch(attended, attended_ref, 10)

    for c in started:
        c.wait_send()
    for slot in range(1, 4):
        for i in range(HEADS_DEV):
            for c in partial_copies(slot, i):
                c.wait_send()
    store_resnet.wait()
    store_attended.wait()


def on_device(
    feature, prev_feature, conv_weight, w_query, w_key, w_value, w_out, prev_keys, prev_values
):
    any_spec = pl.BlockSpec(memory_space=pl.ANY)
    vmem = pltpu.VMEM
    scratch = [
        vmem((4, TOK + 2 * COLS, WIDTH), BF16),
        vmem((TOK, WIDTH), BF16),
        vmem((2, 8, WIDTH), F32),
        vmem((7, 8, WIDTH), F32),
        vmem((3, 8, WIDTH), F32),
        vmem((4, 8, WIDTH), F32),
        vmem((WIDTH, WIDTH), F32),
        vmem((4, 8, WIDTH), F32),
        vmem((2, TOK + 2 * COLS, C // 2), BF16),
        vmem((9, WIDTH, C), BF16),
        vmem((3, WIDTH, C), BF16),
        vmem((3, TOK, WIDTH), F32),
        vmem((TOK, WIDTH), F32),
        vmem((4, TOK, WIDTH), BF16),
        vmem((TOK, C), BF16),
        vmem((4, HEADS_DEV, HEAD_DIM, TOK), BF16),
        vmem((4, HEADS_DEV, TOK, 2 * HEAD_DIM), BF16),
        vmem((HEADS_DEV, 2 * HEAD_DIM, 9 * TOK), BF16),
        vmem((HEADS_DEV, 2 * HEAD_DIM, 9 * TOK), BF16),
        vmem((3, 128, CHUNK), F32),
        vmem((3, 128, 128), F32),
        vmem((4, HEADS_DEV, 72, TOK), F32),
        vmem((3, HEADS_DEV, HEAD_DIM, TOK), BF16),
        vmem((3, HEADS_DEV, HEAD_DIM, TOK), BF16),
        vmem((4, HEADS_DEV, 8, TOK), F32),
        vmem((3, HEADS_DEV, 8, TOK), F32),
        vmem((2, TOK // 2, WIDTH), BF16),
        vmem((2, 2, COLS, WIDTH), BF16),
        vmem((HEADS_DEV, HEAD_DIM, TOK), BF16),
        vmem((4, HEADS_DEV, HEAD_DIM, TOK), BF16),
        vmem((WIDTH, C), BF16),
        vmem((4, WIDTH, WIDTH), BF16),
        vmem((4, WIDTH, WIDTH), BF16),
        vmem((WIDTH, TOK), F32),
        pltpu.SemaphoreType.DMA((SEMS,)),
        pltpu.SemaphoreType.DMA((SEMS,)),
        pltpu.SemaphoreType.DMA((11,)),
    ]
    resnet_out, attended = pl.pallas_call(
        kernel,
        out_shape=(
            jax.ShapeDtypeStruct((TOK, WIDTH), F32),
            jax.ShapeDtypeStruct((WIDTH, TOK), F32),
        ),
        in_specs=[any_spec] * 9,
        out_specs=(any_spec, any_spec),
        scratch_shapes=scratch,
        compiler_params=pltpu.CompilerParams(
            collective_id=0, has_side_effects=True, vmem_limit_bytes=60 * 2**20
        ),
    )(
        feature.reshape(TOK, WIDTH),
        prev_feature.reshape(TOK, WIDTH),
        conv_weight.reshape(9, C, WIDTH).transpose(0, 2, 1),
        w_query.T,
        w_key.T,
        w_value.T,
        w_out,
        prev_keys.T.reshape(HEADS_DEV, HEAD_DIM, TOK),
        prev_values.T.reshape(HEADS_DEV, HEAD_DIM, TOK),
    )
    return (resnet_out.reshape(feature.shape), attended.T)


def solution(mesh):
    placed = (
        P("patch", None, "head"),
        P("patch", None, "head"),
        P(None, None, None, "head"),
        P(None, "head"),
        P(None, "head"),
        P(None, "head"),
        P("head", None),
        P("patch", "head"),
        P("patch", "head"),
    )
    return jax.shard_map(
        on_device,
        mesh=mesh,
        in_specs=placed,
        out_specs=(P("patch", None, "head"), P("patch", "head")),
        check_vma=False,
    )
```

time: 702 us -> 109 us (0.16)
  waiting for transfers between devices: 438 us -> 0 us
  Pallas kernels: 0 us -> 104 us
  matrix products: 70.4 us -> 0 us
  blocking collectives: 70 us -> 0 us
  local copies, waits for them, and re-layouts: 69.2 us -> 3.76 us
  other arithmetic: 31 us -> 0 us
  between operations: 14 us -> 0.64 us
    all_gather x4 -> x0, waiting for transfers between devices: 394 us -> none  [the longest x1 170 us: on_device(): lax.all_gather(prev_values, 'patch', axis=0, tiled=True)]
    pallas_call x0 -> x1, Pallas kernels: none -> 104 us  [on_device(): pl.pallas_call(kernel, out_shape=(jax.ShapeDtypeStruct((TOK, WIDTH), F32)...]
    dot_general x27 -> x0, matrix products: 70.4 us -> none  [the longest x6 25.4 us: attend(): jnp.einsum('qhd,khd->hqk', queries, keys3, preferred_element_type=jnp.flo...]
    psum x1 -> x0, blocking collectives: 70 us -> none  [on_device(): group_sum, group_sq = lax.psum((part_sum, part_sq), 'patch')]
    reduce_scatter x1 -> x0, waiting for transfers between devices: 40.8 us -> none  [on_device(): lax.psum_scatter(partial_out, 'head', scatter_dimension=1, tiled=True)]
    reduce_sum x11 -> x0, other arithmetic: 29.2 us -> none  [the longest x6 25.4 us: attend(): total = total * factor + jnp.sum(expo, axis=-1)]
    all_gather x3 -> x0, local copies, waits for them, and re-layouts: 26.8 us -> none  [the longest x1 11.6 us: on_device(): lax.all_gather(prev_values, 'patch', axis=0, tiled=True)]
    while x8 -> x0, local copies, waits for them, and re-layouts: 23.2 us -> none  [the longest x2 23.2 us: on_device(): lax.scan(step, state, (key_blocks, value_blocks, jnp.arange(blocks, dtype...]
  transfers between devices with their start and end apart: 7 -> 0, of which waited for: 6 -> 0; matrix products, arithmetic and copies ran while one was open for 4% -> 0% of each run, Pallas kernels for 0% -> 0%
where the time goes in v1:
time: 109 us
  Pallas kernels  104 us (95%)
  local copies, waits for them, and re-layouts  3.76 us (3%)
    pallas_call x1, Pallas kernels, on_device(): pl.pallas_call(kernel, out_shape=(jax.ShapeDtypeStruct((TOK, WIDTH), F32)...  104 us
    unnamed x2, local copies, waits for them, and re-layouts  3.76 us

profile of v1, /device:TPU:1, one launch (start us, length us, event | category | flops | bytes accessed | tf_op | source)
XLA Modules:
  0.0 108.6 jit_solution(7811778874736680443)
XLA Ops:
  0.6 104.2 %shard_map.104 = (f32[384,320]{1,0:T(8,128)}, f32[320,384]{1,0:T(8,128)}) custom-call(bf16[384,320]{1,0:T(8,128)(2,1)} %bitcast.22, bf16[384,320]{1,0:T(8,128)(2,1)} %bitcast.23, bf16[9,320,1280]{2,1,0:T(8,128)(2,1)} %bitcast.16, bf16[320,1280]{1,0:T(8,128)(2,1)} %bitcast.17, bf16[320,1280]{1,0:T(8,128)(2,1)} %bitcast.18, bf16[320,1280]{1,0:T(8,128)(2,1)} %bitcast.19, ...), custom_call_target="tpu_custom_call" | custom-call | tf_op jit(solution)/shard_map/pallas_call | solution.py:686
  104.8 1.9 %copy.13 = f32[4,96,320]{2,1,0:T(8,128)} copy(f32[4,96,320]{2,1,0:T(8,128)} %bitcast.20) | data formatting | bytes 983040
  106.7 1.8 %copy.14 = f32[384,320]{0,1:T(8,128)} copy(f32[384,320]{0,1:T(8,128)} %bitcast.21) | data formatting | bytes 983040

commit v2 on v1

--- a/solution.py
+++ b/solution.py
@@ -515,17 +515,19 @@
     def attend(step):
         slot, first = steps[step]
 
-        def body(i, carry):
-            score_rows(slot, first, i, 1)
-            weigh_rows(slot, first, i, 0)
-            score_rows(slot, first, i, 2)
-            weigh_rows(slot, first, i, 1)
-            score_rows(slot, first, i + 1, 0)
-            weigh_rows(slot, first, i, 2)
-            send_partial(slot, first, i)
+        def body(pair, carry):
+            for i in (2 * pair, 2 * pair + 1):
+                score_rows(slot, first, i, 1)
+                weigh_rows(slot, first, i, 0)
+                score_rows(slot, first, i, 2)
+                weigh_rows(slot, first, i, 1)
+                score_rows(slot, first, i + 1, 0)
+                weigh_rows(slot, first, i, 2)
+            for i in (2 * pair, 2 * pair + 1):
+                send_partial(slot, first, i)
             return carry
 
-        lax.fori_loop(0, HEADS_DEV - 1, body, 0)
+        lax.fori_loop(0, (HEADS_DEV - 1) // 2, body, 0)
 
     def attend_head(slot, first, i, following):
         def body(unused, carry):

time: 109 us -> 107 us (0.982)
  Pallas kernels: 104 us -> 102 us
    pallas_call x1, Pallas kernels: 104 us -> 102 us  [on_device(): pl.pallas_call(kernel, out_shape=(jax.ShapeDtypeStruct((TOK, WIDTH), F32)...]
where the time goes in v2:
time: 107 us
  Pallas kernels  102 us (95%)
  local copies, waits for them, and re-layouts  3.76 us (4%)
    pallas_call x1, Pallas kernels, on_device(): pl.pallas_call(kernel, out_shape=(jax.ShapeDtypeStruct((TOK, WIDTH), F32)...  102 us
    unnamed x2, local copies, waits for them, and re-layouts  3.76 us

profile of v2, /device:TPU:1, one launch (start us, length us, event | category | flops | bytes accessed | tf_op | source)
XLA Modules:
  0.0 106.9 jit_solution(300911794302911222)
XLA Ops:
  0.6 102.5 %shard_map.104 = (f32[384,320]{1,0:T(8,128)}, f32[320,384]{1,0:T(8,128)}) custom-call(bf16[384,320]{1,0:T(8,128)(2,1)} %bitcast.22, bf16[384,320]{1,0:T(8,128)(2,1)} %bitcast.23, bf16[9,320,1280]{2,1,0:T(8,128)(2,1)} %bitcast.16, bf16[320,1280]{1,0:T(8,128)(2,1)} %bitcast.17, bf16[320,1280]{1,0:T(8,128)(2,1)} %bitcast.18, bf16[320,1280]{1,0:T(8,128)(2,1)} %bitcast.19, ...), custom_call_target="tpu_custom_call" | custom-call | tf_op jit(solution)/shard_map/pallas_call | solution.py:688
  103.1 1.9 %copy.13 = f32[4,96,320]{2,1,0:T(8,128)} copy(f32[4,96,320]{2,1,0:T(8,128)} %bitcast.20) | data formatting | bytes 983040
  105.1 1.8 %copy.14 = f32[384,320]{0,1:T(8,128)} copy(f32[384,320]{0,1:T(8,128)} %bitcast.21) | data formatting | bytes 983040
